TPU v7x, 32 devices: a whole 2x2x4 slice. The times are simulated.
32 devices in a mesh: chan: 8 (over y, x, core), win: 4 (over z).
Axes of the slice: x: 2, y: 2, z: 4, core: 2. Of those that a mesh axis runs over, the one named last changes fastest.
Arguments:
- spectra: float32 [4, 256, 2, 4096], P('win', 'chan'), may hold values from -2000 to 2000
- sources: int32 [2, 8], replicated, may hold values from 0 to 255, as said below
- window_valid: int32 [4, 256], P('win', 'chan'), may hold values 0 or 1
Outputs:
- correlations: float32 [2, 8, 256, 256], P(None, 'win', 'chan')
Inputs may be any that keep to these rules, and one draw needn't show every extreme that they name: sources[t, s] is a channel of owner s, that is between (s) * 32 and (s + 1) * 32 - 1; the entries of one turn are distinct.
All inputs are finite; a program needn't handle non-finite values. No bound on the sum of `window_valid` on one device may be relied on, other than what follows from the above.
Results may differ from a plain program's by a relative error of at most 0.0022.
Values may be sent and summed in bfloat16 or wider, within the bound.
A program may use at most 64 MiB of HBM per device.

v0:
```python
import math
import jax
import jax.numpy as jnp
from jax import lax
from jax.sharding import PartitionSpec as P

LAGS = 256


def whiten(spectra, window_valid):
    mean_power = jnp.mean(spectra * spectra, axis=(2, 3), keepdims=True)
    valid_flags = window_valid.astype(jnp.float32)[:, :, None, None]
    whitened = valid_flags * spectra / jnp.sqrt(mean_power + 1e-05)
    return whitened.astype(jnp.bfloat16).reshape(
        spectra.shape[0], spectra.shape[1], 2 * spectra.shape[3]
    )


def build_table(freq_count, lag_count):
    shifts = jnp.arange(lag_count, dtype=jnp.int32) - lag_count // 2
    freq_bins = jnp.arange(freq_count, dtype=jnp.int32)
    phase_index = freq_bins[:, None] * shifts[None, :] % (2 * freq_count)
    angles = phase_index.astype(jnp.float32) * (math.pi / freq_count)
    return jnp.concatenate([jnp.cos(angles), -jnp.sin(angles)], axis=0).astype(jnp.bfloat16)


def cross_block(source_piece, receivers, trig_table):
    half_width = receivers.shape[2] // 2
    src_real = source_piece[:, :, None, :half_width].astype(jnp.float32)
    src_imag = source_piece[:, :, None, half_width:].astype(jnp.float32)
    rec_real = receivers[:, None, :, :half_width].astype(jnp.float32)
    rec_imag = receivers[:, None, :, half_width:].astype(jnp.float32)
    cross_real = (src_real * rec_real + src_imag * rec_imag).astype(jnp.bfloat16)
    cross_imag = (src_imag * rec_real - src_real * rec_imag).astype(jnp.bfloat16)
    cross_both = jnp.concatenate([cross_real, cross_imag], axis=-1)
    lag_values = jnp.dot(
        cross_both.reshape(-1, 2 * half_width), trig_table, preferred_element_type=jnp.float32
    )
    lag_values = lag_values.reshape(
        source_piece.shape[0], source_piece.shape[1], receivers.shape[1], -1
    )
    return jnp.sum(lag_values, axis=0)


def local(spectra, sources, window_valid):
    whitened = whiten(spectra, window_valid)
    win_local = whitened.shape[0]
    chan_local = whitened.shape[1]
    freq_count = spectra.shape[3]
    turn_count = sources.shape[0]
    trig_table = build_table(freq_count, LAGS)
    norm_scale = 1.0 / math.sqrt(freq_count * win_local * lax.axis_size("win"))
    own_count = sources.shape[1] // lax.axis_size("chan")
    owner_index = lax.axis_index("chan")
    local_rows = (
        lax.dynamic_slice_in_dim(sources, owner_index * own_count, own_count, 1)
        - owner_index * chan_local
    )
    picked = jnp.take(whitened, local_rows.reshape(-1), axis=1).reshape(
        win_local, turn_count, own_count, 2 * freq_count
    )
    everything = lax.all_gather(picked, "chan", axis=2, tiled=True)
    per_turn = [everything[:, turn_index] for turn_index in range(turn_count)]
    results = []
    for gathered in per_turn:
        share_rows = gathered.shape[1] // lax.axis_size("win")

        def stack_term(first_row, row_count, gathered=gathered):
            sub_size = math.gcd(row_count, 8)
            sub_number = row_count // sub_size
            sub_blocks = gathered.reshape(
                win_local, sub_number, sub_size, 2 * freq_count
            ).transpose(1, 0, 2, 3)
            partial_value = lax.map(
                lambda source_piece: cross_block(source_piece, whitened, trig_table), sub_blocks
            )
            return partial_value.reshape(row_count, chan_local, -1)

        stacked = lax.psum_scatter(
            stack_term(jnp.int32(0), share_rows * lax.axis_size("win")),
            "win",
            scatter_dimension=0,
            tiled=True,
        )
        results.append(stacked * norm_scale)
    return jnp.stack(results, axis=0)


def solution(mesh):
    placed = (P("win", "chan", None, None), P(), P("win", "chan"))
    return jax.shard_map(
        local, mesh=mesh, in_specs=placed, out_specs=P(None, "win", "chan", None), check_vma=False
    )
```

profile of v0, /device:TPU:0, one launch (start us, length us, event | category | flops | bytes accessed | tf_op | source)
XLA Modules:
  0.0 96.3 jit_solution(6179811309796717721)
XLA Ops:
  6.5 0.0 reduce-scatter.3.cloned.1.call-start
  6.5 0.9 and_reduce_fusion
  7.4 0.1 reduce.2
  7.5 1.9 %multiply_reduce_fusion = f32[32]{0:T(128)S(1)} fusion(f32[1,32,2,4096]{3,2,1,0:T(2,128)} %param.3), kind=kLoop, calls=%fused_computation.25 | loop fusion | flops 524256 | bytes 1048704 | tf_op jit(solution)/shard_map/reduce_sum | solution.py:11
  9.4 0.7 convert_bitcast_fusion
  10.1 1.9 %fusion.12 = bf16[1,32,2,4096]{3,2,1,0:T(2,128)(2,1)S(1)} fusion(f32[1,32,2,4096]{3,2,1,0:T(2,128)} %param.3, f32[32]{0:T(128)S(1)} %add_sqrt_fusion, f32[32]{0:T(128)S(1)} %convert_bitcast_fusion), kind=kLoop, calls=%fused_computation.27 | loop fusion | flops 786432 | bytes 1573120 | tf_op jit(solution)/shard_map/convert_element_type | solution.py:14
  12.0 0.4 reshape.261
  12.4 0.3 copy.9
  12.7 0.6 gather_fusion
  13.3 0.1 fusion.19
  13.4 10.8 %all_gather.3 = bf16[1,2,8,8192]{3,1,0,2:T(2,128)(2,1)S(1)} all-gather(bf16[1,2,1,8192]{3,1,0,2:T(2,128)(2,1)S(1)} %fusion.19), channel_id=1, replica_groups=mesh['chan'=8,'win'=4] {'chan'}, dimensions={2}, use_global_device_ids=true | all-gather | bytes 294912 | tf_op jit(solution)/shard_map/all_gather | solution.py:62
  24.2 0.5 fusion.22
  24.6 0.3 copy_bitcast_fusion
  25.0 0.1 fusion.14
  25.1 17.0 %cosine_convert_fusion = (bf16[4096,256]{1,0:T(8,128)(2,1)S(1)}, bf16[4096,256]{1,0:T(8,128)(2,1)S(1)}) fusion(s32[256]{0:T(256)S(1)} %iota_add_fusion), kind=kLoop, calls=%fused_computation.19 | loop fusion | flops 17825792 | bytes 4195328 | tf_op jit(solution)/shard_map/convert.6
  42.0 0.0 copy-start
  42.1 0.0 copy-start.1
  42.1 3.5 %add_convert_fusion.1 = (bf16[1,8,32,4096]{3,2,1,0:T(8,128)(2,1)S(1)}, bf16[1,8,32,4096]{3,2,1,0:T(8,128)(2,1)S(1)}, bf16[1,8,32,4096]{3,2,1,0:T(8,128)(2,1)S(1)}, bf16[1,8,32,4096]{3,2,1,0:T(8,128)(2,1)}) fusion(f32[32,4096]{1,0:T(8,128)S(1)} %get-tuple-element.44, f32[8,4096]{1,0:T(8,128)S(1)} %get-tuple-element.48, f32[32,4096]{1,0:T(8,128)S(1)} %get-tuple-element.42, ...), kind=kLoop, calls=%fused_computation.23 | loop fusion | flops 16777216 | bytes 9961472 | tf_op jit(solution)/shard_map/while/body/eval_jaxpr/convert_element_type | solution.py:33
  45.6 0.0 copy-done
  45.6 0.0 copy-done.1
  45.6 1.9 %fusion.3 = f32[8,32,256]{2,1,0:T(8,128)} fusion(bf16[1,8,32,4096]{3,2,1,0:T(8,128)(2,1)S(1)} %get-tuple-element.31, bf16[1,8,32,4096]{3,2,1,0:T(8,128)(2,1)S(1)} %get-tuple-element.30, bf16[4096,256]{1,0:T(8,128)(2,1)S(1)} %get-tuple-element.52, bf16[4096,256]{1,0:T(8,128)(2,1)S(1)} %get-tuple-element.51), kind=kOutput, calls=%fused_computation.8 | convolution fusion | flops 1090519040 | bytes 8650752 | tf_op jit(solution)/shard_map/while/body/eval_jaxpr/dot_general | solution.py:36
  47.5 0.0 reduce-scatter.3.cloned.1.call-update
  47.6 0.0 reduce-scatter.5.cloned.1.call-start
  47.6 4.8 %fusion.6 = f32[8,32,256]{2,1,0:T(8,128)} fusion(bf16[1,8,32,4096]{3,2,1,0:T(8,128)(2,1)S(1)} %get-tuple-element.34, bf16[1,8,32,4096]{3,2,1,0:T(8,128)(2,1)} %get-tuple-element.40, bf16[4096,256]{1,0:T(8,128)(2,1)} %copy-done.1, bf16[4096,256]{1,0:T(8,128)(2,1)} %copy-done), kind=kOutput, calls=%fused_computation.13 | convolution fusion | flops 1090519040 | bytes 8650752 | tf_op jit(solution)/shard_map/while/body/eval_jaxpr/dot_general | solution.py:36
  52.4 0.0 reduce-scatter.5.cloned.1.call-update
  52.5 15.2 %reduce-scatter.3.cloned.1.call-done = f32[2,32,256]{2,1,0:T(8,128)} async-done(((f32[8,32,256]{2,1,0:T(8,128)}), f32[2,32,256]{2,1,0:T(8,128)}) %reduce-scatter.3.cloned.1.call-update) | async-done | bytes 65552 | tf_op jit(solution)/shard_map/reduce_scatter | solution.py:79
  67.6 0.8 multiply_bitcast_fusion.1
  68.5 19.5 %reduce-scatter.5.cloned.1.call-done = f32[2,32,256]{2,1,0:T(8,128)} async-done(((f32[8,32,256]{2,1,0:T(8,128)}), f32[2,32,256]{2,1,0:T(8,128)}) %reduce-scatter.5.cloned.1.call-update) | async-done | bytes 65552 | tf_op jit(solution)/shard_map/reduce_scatter | solution.py:79
  87.9 0.8 multiply_bitcast_fusion
  88.8 0.7 pad_maximum_fusion
  (5 shorter events, 0.1 us)
Async XLA Ops:
  6.5 61.1 %reduce-scatter.3.cloned.1.call-start = ((), (), s32[]{:S(2)}) async-start(), calls=%async_computation.2 | async-start | bytes 327680 | tf_op jit(solution)/shard_map/reduce_scatter | solution.py:79
  42.0 3.5 %copy-start = (bf16[4096,256]{1,0:T(8,128)(2,1)}, bf16[4096,256]{1,0:T(8,128)(2,1)S(1)}, u32[]{:S(2)}) copy-start(bf16[4096,256]{1,0:T(8,128)(2,1)S(1)} %get-tuple-element.51) | copy-start | bytes 6291460
  42.1 3.5 %copy-start.1 = (bf16[4096,256]{1,0:T(8,128)(2,1)}, bf16[4096,256]{1,0:T(8,128)(2,1)S(1)}, u32[]{:S(2)}) copy-start(bf16[4096,256]{1,0:T(8,128)(2,1)S(1)} %get-tuple-element.52) | copy-start | bytes 6291460
  47.6 40.4 %reduce-scatter.5.cloned.1.call-start = ((), (), s32[]{:S(2)}) async-start(), calls=%async_computation.3 | async-start | bytes 327680 | tf_op jit(solution)/shard_map/reduce_scatter | solution.py:79
Sparse Core Ops, SparseCore 0:
  47.7 19.8 reduce-scatter.2
  70.0 17.9 reduce-scatter.4
where the time goes:
time: 96.6 us; the launch traced here: 96.3 us
  waiting for transfers between devices  34.7 us (36%)
  other arithmetic  28.5 us (30%)
  between operations  13.5 us (14%)
  blocking collectives  10.8 us (11%)
  matrix products  6.77 us (7%)
  local copies, waits for them, and re-layouts  2.06 us (2%)
    reduce_scatter x2, waiting for transfers between devices, local(): lax.psum_scatter(stack_term(jnp.int32(0), share_rows * lax.axis_size('win...  34.6 us
    another operation x1, other arithmetic  17 us
    all_gather x1, blocking collectives, local(): everything = lax.all_gather(picked, 'chan', axis=2, tiled=True)  10.8 us
    dot_general x2, matrix products, cross_block(): jnp.dot(cross_both.reshape(-1, 2 * half_width), trig_table, preferred_ele...  6.77 us
    convert_element_type x1, other arithmetic, cross_block(): (src_real * rec_real + src_imag * rec_imag).astype(jnp.bfloat16)  3.51 us
    another operation x3, other arithmetic, local(): return jnp.stack(results, axis=0)  2.35 us
  transfers between devices with their start and end apart: 2, of which 2 were waited for; matrix products, arithmetic and copies ran while one was open for 6% of the time, Pallas kernels for 0%

commit v1 on v0

--- a/solution.py
+++ b/solution.py
@@ -5,6 +5,24 @@
 from jax.sharding import PartitionSpec as P
 
 LAGS = 256
+
+
+def collect(shard, axis, dim):
+    ways, here, step = (lax.axis_size(axis), lax.axis_index(axis), shard.shape[dim])
+    lengths = [n * ways if d == dim else n for d, n in enumerate(shard.shape)]
+    full = lax.dynamic_update_slice_in_dim(
+        jnp.zeros(lengths, shard.dtype), shard, here * step, axis=dim
+    )
+    going_up = going_down = shard
+    for far in range(1, ways // 2 + 1):
+        going_up = lax.ppermute(going_up, axis, [(d, (d + 1) % ways) for d in range(ways)])
+        full = lax.dynamic_update_slice_in_dim(full, going_up, (here - far) % ways * step, axis=dim)
+        if 2 * far < ways:
+            going_down = lax.ppermute(going_down, axis, [(d, (d - 1) % ways) for d in range(ways)])
+            full = lax.dynamic_update_slice_in_dim(
+                full, going_down, (here + far) % ways * step, axis=dim
+            )
+    return full
 
 
 def whiten(spectra, window_valid):
@@ -59,7 +77,7 @@
     picked = jnp.take(whitened, local_rows.reshape(-1), axis=1).reshape(
         win_local, turn_count, own_count, 2 * freq_count
     )
-    everything = lax.all_gather(picked, "chan", axis=2, tiled=True)
+    everything = collect(picked, "chan", 2)
     per_turn = [everything[:, turn_index] for turn_index in range(turn_count)]
     results = []
     for gathered in per_turn:

time: 96.6 us -> 109 us (1.13)
  blocking collectives: 10.8 us -> 0 us
  starting transfers between devices: 0.04 us -> 8.72 us
  local copies, waits for them, and re-layouts: 2.06 us -> 9.89 us
  waiting for transfers between devices: 34.7 us -> 40.1 us
  other arithmetic: 28.5 us -> 29.8 us
    all_gather x1 -> x0, blocking collectives: 10.8 us -> none  [local(): everything = lax.all_gather(picked, 'chan', axis=2, tiled=True)]
    ppermute x0 -> x7, starting transfers between devices: none -> 8.67 us  [the longest x3 8.16 us: collect(): lax.ppermute(going_down, axis, [(d, (d - 1) % ways) for d in range(ways)])]
    dynamic_update_slice x0 -> x8, local copies, waits for them, and re-layouts: none -> 8.13 us  [the longest x4 4.07 us: collect(): lax.dynamic_update_slice_in_dim(full, going_up, (here - far) % ways * ste...]
    ppermute x0 -> x7, waiting for transfers between devices: none -> 3.13 us  [the longest x4 3.07 us: collect(): lax.ppermute(going_up, axis, [(d, (d + 1) % ways) for d in range(ways)])]
    reduce_scatter x2, waiting for transfers between devices: 34.6 us -> 36.9 us  [local(): lax.psum_scatter(stack_term(jnp.int32(0), share_rows * lax.axis_size('win...]
    another operation x1, other arithmetic: 17 us -> 18.2 us
  transfers between devices with their start and end apart: 2 -> 9, of which waited for: 2 -> 5; matrix products, arithmetic and copies ran while one was open for 6% -> 29% of each run, Pallas kernels for 0% -> 0%
where the time goes in v1:
time: 109 us
  waiting for transfers between devices  40.1 us (37%)
  other arithmetic  29.8 us (27%)
  between operations  13.8 us (13%)
  local copies, waits for them, and re-layouts  9.89 us (9%)
  starting transfers between devices  8.72 us (8%)
  matrix products  6.77 us (6%)
    reduce_scatter x2, waiting for transfers between devices, local(): lax.psum_scatter(stack_term(jnp.int32(0), share_rows * lax.axis_size('win...  36.9 us
    another operation x1, other arithmetic  18.2 us
    ppermute x3, starting transfers between devices, collect(): lax.ppermute(going_down, axis, [(d, (d - 1) % ways) for d in range(ways)])  8.16 us
    dot_general x2, matrix products, cross_block(): jnp.dot(cross_both.reshape(-1, 2 * half_width), trig_table, preferred_ele...  6.77 us
    dynamic_update_slice x4, local copies, waits for them, and re-layouts, collect(): lax.dynamic_update_slice_in_dim(full, going_up, (here - far) % ways * ste...  4.07 us
    convert_element_type x1, other arithmetic, cross_block(): (src_real * rec_real + src_imag * rec_imag).astype(jnp.bfloat16)  3.59 us
    ppermute x4, waiting for transfers between devices, collect(): lax.ppermute(going_up, axis, [(d, (d + 1) % ways) for d in range(ways)])  3.07 us
    dynamic_update_slice x3, local copies, waits for them, and re-layouts, collect(): lax.dynamic_update_slice_in_dim(full, going_down, (here + far) % ways * s...  3.05 us
  transfers between devices with their start and end apart: 9, of which 5 were waited for; matrix products, arithmetic and copies ran while one was open for 29% of the time, Pallas kernels for 0%

profile of v1, /device:TPU:0, one launch (start us, length us, event | category | flops | bytes accessed | tf_op | source)
XLA Modules:
  0.0 109.0 jit_solution(11735645967822483)
XLA Ops:
  6.5 0.9 fusion.21
  7.4 1.9 %multiply_reduce_fusion = f32[32]{0:T(128)S(1)} fusion(f32[1,32,2,4096]{3,2,1,0:T(2,128)} %param.3), kind=kLoop, calls=%fused_computation.25 | loop fusion | flops 524256 | bytes 1048704 | tf_op jit(solution)/shard_map/reduce_sum | solution.py:29
  9.3 0.7 convert_bitcast_fusion
  10.0 1.9 %fusion.12 = bf16[1,32,2,4096]{3,2,1,0:T(2,128)(2,1)S(1)} fusion(f32[1,32,2,4096]{3,2,1,0:T(2,128)} %param.3, f32[32]{0:T(128)S(1)} %add_sqrt_fusion, f32[32]{0:T(128)S(1)} %convert_bitcast_fusion), kind=kLoop, calls=%fused_computation.27 | loop fusion | flops 786432 | bytes 1573120 | tf_op jit(solution)/shard_map/convert_element_type | solution.py:32
  11.9 0.3 copy.12
  12.2 0.1 and_reduce_fusion
  12.3 0.6 gather_fusion
  12.9 0.1 broadcast_select_fusion
  13.0 0.5 collective-permute-start
  13.5 2.9 %collective-permute-start.1 = (bf16[1,2,1,8192]{3,1,2,0:T(2,128)(2,1)S(1)}, bf16[1,2,1,8192]{3,1,2,0:T(2,128)(2,1)S(1)}, u32[]{:S(2)}, u32[]{:S(2)}) collective-permute-start(bf16[1,2,1,8192]{3,1,2,0:T(2,128)(2,1)S(1)} %broadcast_select_fusion), channel_id=1, source_target_pairs={{0,28},{4,0},{8,4},{12,8},{16,12},{20,16},{24,20},{28,24},{1,29},{... | collective-permute-start | bytes 98312 | tf_op jit(solution)/shard_map/ppermute | solution.py:21
  16.4 1.5 %collective-permute-done = bf16[1,2,1,8192]{3,1,2,0:T(2,128)(2,1)S(1)} collective-permute-done((bf16[1,2,1,8192]{3,1,2,0:T(2,128)(2,1)S(1)}, bf16[1,2,1,8192]{3,1,2,0:T(2,128)(2,1)S(1)}, u32[]{:S(2)}, u32[]{:S(2)}) %collective-permute-start) | collective-permute-done | bytes 32800 | tf_op jit(solution)/shard_map/ppermute | solution.py:18
  18.0 2.6 %collective-permute-start.3 = (bf16[1,2,1,8192]{3,1,2,0:T(2,128)(2,1)S(1)}, bf16[1,2,1,8192]{3,1,2,0:T(2,128)(2,1)S(1)}, u32[]{:S(2)}, u32[]{:S(2)}) collective-permute-start(bf16[1,2,1,8192]{3,1,2,0:T(2,128)(2,1)S(1)} %collective-permute-done.1), channel_id=1, source_target_pairs={{0,28},{4,0},{8,4},{12,8},{16,12},{20,16},{24,20},{28,24},{1,29},{... | collective-permute-start | bytes 98312 | tf_op jit(solution)/shard_map/ppermute | solution.py:21
  20.7 1.5 %collective-permute-done.2 = bf16[1,2,1,8192]{3,1,2,0:T(2,128)(2,1)S(1)} collective-permute-done((bf16[1,2,1,8192]{3,1,2,0:T(2,128)(2,1)S(1)}, bf16[1,2,1,8192]{3,1,2,0:T(2,128)(2,1)S(1)}, u32[]{:S(2)}, u32[]{:S(2)}) %collective-permute-start.2) | collective-permute-done | bytes 32800 | tf_op jit(solution)/shard_map/ppermute | solution.py:18
  22.2 18.2 %cosine_convert_fusion = (bf16[4096,256]{1,0:T(8,128)(2,1)}, bf16[4096,256]{1,0:T(8,128)(2,1)}) fusion(s32[256]{0:T(256)S(1)} %iota_add_fusion), kind=kLoop, calls=%fused_computation.19 | loop fusion | flops 17825792 | bytes 4195328 | tf_op jit(solution)/shard_map/convert.6
  40.4 0.4 reshape.261
  40.8 2.6 %collective-permute-start.5 = (bf16[1,2,1,8192]{3,1,2,0:T(2,128)(2,1)S(1)}, bf16[1,2,1,8192]{3,1,2,0:T(2,128)(2,1)S(1)}, u32[]{:S(2)}, u32[]{:S(2)}) collective-permute-start(bf16[1,2,1,8192]{3,1,2,0:T(2,128)(2,1)S(1)} %collective-permute-done.3), channel_id=1, source_target_pairs={{0,28},{4,0},{8,4},{12,8},{16,12},{20,16},{24,20},{28,24},{1,29},{... | collective-permute-start | bytes 98312 | tf_op jit(solution)/shard_map/ppermute | solution.py:21
  43.7 1.0 dynamic_update_slice.29
  44.8 1.0 dynamic_update_slice.30
  45.9 1.0 dynamic_update_slice.31
  47.0 1.0 dynamic_update_slice.32
  48.1 1.0 dynamic_update_slice.33
  49.2 1.0 dynamic_update_slice.34
  50.3 1.0 dynamic_update_slice.35
  51.4 1.0 dynamic_update_slice.36
  52.5 3.6 %add_convert_fusion.1 = (bf16[1,8,32,4096]{3,2,1,0:T(8,128)(2,1)S(1)}, bf16[1,8,32,4096]{3,2,1,0:T(8,128)(2,1)S(1)}, bf16[1,8,32,4096]{3,2,1,0:T(8,128)(2,1)S(1)}, bf16[1,8,32,4096]{3,2,1,0:T(8,128)(2,1)}) fusion(f32[32,4096]{1,0:T(8,128)S(1)} %get-tuple-element.44, f32[8,4096]{1,0:T(8,128)S(1)} %get-tuple-element.53, f32[32,4096]{1,0:T(8,128)S(1)} %get-tuple-element.42, ...), kind=kLoop, calls=%fused_computation.23 | loop fusion | flops 16777216 | bytes 9961472 | tf_op jit(solution)/shard_map/while/body/eval_jaxpr/convert_element_type | solution.py:51
  56.1 2.0 %fusion.3 = f32[8,32,256]{2,1,0:T(8,128)} fusion(bf16[1,8,32,4096]{3,2,1,0:T(8,128)(2,1)S(1)} %get-tuple-element.31, bf16[1,8,32,4096]{3,2,1,0:T(8,128)(2,1)S(1)} %get-tuple-element.30, bf16[4096,256]{1,0:T(8,128)(2,1)S(1)} %copy-done.1, bf16[4096,256]{1,0:T(8,128)(2,1)S(1)} %copy-done), kind=kOutput, calls=%fused_computation.8 | convolution fusion | flops 1090519040 | bytes 8650752 | tf_op jit(solution)/shard_map/while/body/eval_jaxpr/dot_general | solution.py:54
  58.1 4.8 %fusion.6 = f32[8,32,256]{2,1,0:T(8,128)} fusion(bf16[1,8,32,4096]{3,2,1,0:T(8,128)(2,1)S(1)} %get-tuple-element.34, bf16[1,8,32,4096]{3,2,1,0:T(8,128)(2,1)} %get-tuple-element.40, bf16[4096,256]{1,0:T(8,128)(2,1)} %get-tuple-element.52, bf16[4096,256]{1,0:T(8,128)(2,1)} %get-tuple-element.51), kind=kOutput, calls=%fused_computation.13 | convolution fusion | flops 1090519040 | bytes 8650752 | tf_op jit(solution)/shard_map/while/body/eval_jaxpr/dot_general | solution.py:54
  62.9 17.4 %reduce-scatter.3.cloned.1.call-done = f32[2,32,256]{2,1,0:T(8,128)} async-done(((f32[8,32,256]{2,1,0:T(8,128)}), f32[2,32,256]{2,1,0:T(8,128)}) %reduce-scatter.3.cloned.1.call-update) | async-done | bytes 65552 | tf_op jit(solution)/shard_map/reduce_scatter | solution.py:97
  80.4 0.8 multiply_bitcast_fusion.1
  81.2 19.5 %reduce-scatter.5.cloned.1.call-done = f32[2,32,256]{2,1,0:T(8,128)} async-done(((f32[8,32,256]{2,1,0:T(8,128)}), f32[2,32,256]{2,1,0:T(8,128)}) %reduce-scatter.5.cloned.1.call-update) | async-done | bytes 65552 | tf_op jit(solution)/shard_map/reduce_scatter | solution.py:97
  100.7 0.8 multiply_bitcast_fusion
  101.5 0.7 pad_maximum_fusion
  (31 shorter events, 0.7 us)
Async XLA Ops:
  6.5 73.9 %reduce-scatter.3.cloned.1.call-start = ((), (), s32[]{:S(2)}) async-start(), calls=%async_computation.2 | async-start | bytes 327680 | tf_op jit(solution)/shard_map/reduce_scatter | solution.py:97
  13.0 5.0 %collective-permute-start = (bf16[1,2,1,8192]{3,1,2,0:T(2,128)(2,1)S(1)}, bf16[1,2,1,8192]{3,1,2,0:T(2,128)(2,1)S(1)}, u32[]{:S(2)}, u32[]{:S(2)}) collective-permute-start(bf16[1,2,1,8192]{3,1,2,0:T(2,128)(2,1)S(1)} %broadcast_select_fusion), channel_id=1, source_target_pairs={{0,4},{4,8},{8,12},{12,16},{16,20},{20,24},{24,28},{28,0},{1,5},{5... | collective-permute-start | bytes 98312 | tf_op jit(solution)/shard_map/ppermute | solution.py:18
  13.5 4.5 %collective-permute-start.1 = (bf16[1,2,1,8192]{3,1,2,0:T(2,128)(2,1)S(1)}, bf16[1,2,1,8192]{3,1,2,0:T(2,128)(2,1)S(1)}, u32[]{:S(2)}, u32[]{:S(2)}) collective-permute-start(bf16[1,2,1,8192]{3,1,2,0:T(2,128)(2,1)S(1)} %broadcast_select_fusion), channel_id=1, source_target_pairs={{0,28},{4,0},{8,4},{12,8},{16,12},{20,16},{24,20},{28,24},{1,29},{... | collective-permute-start | bytes 98312 | tf_op jit(solution)/shard_map/ppermute | solution.py:21
  18.0 4.2 %collective-permute-start.2 = (bf16[1,2,1,8192]{3,1,2,0:T(2,128)(2,1)S(1)}, bf16[1,2,1,8192]{3,1,2,0:T(2,128)(2,1)S(1)}, u32[]{:S(2)}, u32[]{:S(2)}) collective-permute-start(bf16[1,2,1,8192]{3,1,2,0:T(2,128)(2,1)S(1)} %collective-permute-done), channel_id=1, source_target_pairs={{0,4},{4,8},{8,12},{12,16},{16,20},{20,24},{24,28},{28,0},{1,5},{5... | collective-permute-start | bytes 98312 | tf_op jit(solution)/shard_map/ppermute | solution.py:18
  18.0 22.8 %collective-permute-start.3 = (bf16[1,2,1,8192]{3,1,2,0:T(2,128)(2,1)S(1)}, bf16[1,2,1,8192]{3,1,2,0:T(2,128)(2,1)S(1)}, u32[]{:S(2)}, u32[]{:S(2)}) collective-permute-start(bf16[1,2,1,8192]{3,1,2,0:T(2,128)(2,1)S(1)} %collective-permute-done.1), channel_id=1, source_target_pairs={{0,28},{4,0},{8,4},{12,8},{16,12},{20,16},{24,20},{28,24},{1,29},{... | collective-permute-start | bytes 98312 | tf_op jit(solution)/shard_map/ppermute | solution.py:21
  22.2 21.2 %collective-permute-start.4 = (bf16[1,2,1,8192]{3,1,2,0:T(2,128)(2,1)S(1)}, bf16[1,2,1,8192]{3,1,2,0:T(2,128)(2,1)S(1)}, u32[]{:S(2)}, u32[]{:S(2)}) collective-permute-start(bf16[1,2,1,8192]{3,1,2,0:T(2,128)(2,1)S(1)} %collective-permute-done.2), channel_id=1, source_target_pairs={{0,4},{4,8},{8,12},{12,16},{16,20},{20,24},{24,28},{28,0},{1,5},{5... | collective-permute-start | bytes 98312 | tf_op jit(solution)/shard_map/ppermute | solution.py:18
  40.8 9.4 %collective-permute-start.5 = (bf16[1,2,1,8192]{3,1,2,0:T(2,128)(2,1)S(1)}, bf16[1,2,1,8192]{3,1,2,0:T(2,128)(2,1)S(1)}, u32[]{:S(2)}, u32[]{:S(2)}) collective-permute-start(bf16[1,2,1,8192]{3,1,2,0:T(2,128)(2,1)S(1)} %collective-permute-done.3), channel_id=1, source_target_pairs={{0,28},{4,0},{8,4},{12,8},{16,12},{20,16},{24,20},{28,24},{1,29},{... | collective-permute-start | bytes 98312 | tf_op jit(solution)/shard_map/ppermute | solution.py:21
  43.4 7.9 %collective-permute-start.6 = (bf16[1,2,1,8192]{3,1,2,0:T(2,128)(2,1)S(1)}, bf16[1,2,1,8192]{3,1,2,0:T(2,128)(2,1)S(1)}, u32[]{:S(2)}, u32[]{:S(2)}) collective-permute-start(bf16[1,2,1,8192]{3,1,2,0:T(2,128)(2,1)S(1)} %collective-permute-done.4), channel_id=1, source_target_pairs={{0,4},{4,8},{8,12},{12,16},{16,20},{20,24},{24,28},{28,0},{1,5},{5... | collective-permute-start | bytes 98312 | tf_op jit(solution)/shard_map/ppermute | solution.py:18
  52.5 3.6 %copy-start = (bf16[4096,256]{1,0:T(8,128)(2,1)S(1)}, bf16[4096,256]{1,0:T(8,128)(2,1)}, u32[]{:S(2)}) copy-start(bf16[4096,256]{1,0:T(8,128)(2,1)} %get-tuple-element.51) | copy-start | bytes 6291460
  52.5 3.6 %copy-start.1 = (bf16[4096,256]{1,0:T(8,128)(2,1)S(1)}, bf16[4096,256]{1,0:T(8,128)(2,1)}, u32[]{:S(2)}) copy-start(bf16[4096,256]{1,0:T(8,128)(2,1)} %get-tuple-element.52) | copy-start | bytes 6291460
  58.1 42.6 %reduce-scatter.5.cloned.1.call-start = ((), (), s32[]{:S(2)}) async-start(), calls=%async_computation.3 | async-start | bytes 327680 | tf_op jit(solution)/shard_map/reduce_scatter | solution.py:97
Sparse Core Ops, SparseCore 0:
  58.2 22.1 reduce-scatter.2
  82.7 17.9 reduce-scatter.4
